TPU v7x, 32 devices: a whole 2x2x4 slice. The times are simulated.
32 devices in a mesh: kpt: 2 (over x), row: 16 (over z, y, core).
Axes of the slice: x: 2, y: 2, z: 4, core: 2. Of those that a mesh axis runs over, the one named last changes fastest.
Arguments:
- orbitals_zero: float32 [32768, 1024], P(('kpt', 'row')), parts along dimension 0, may hold values from -0.046875 to 0.046875
- orbitals_one: float32 [32768, 1024], P(('kpt', 'row')), parts along dimension 0, may hold values from -0.046875 to 0.046875
- correlation_zero: float32 [2048, 1024], P('kpt'), parts along dimension 0, as said below
- correlation_one: float32 [2048, 1024], P('kpt'), parts along dimension 0, as said below
- cotangent: float32 [32768, 1024], P(('kpt', 'row')), parts along dimension 0, may hold values from -6 to 6
Outputs:
- orbital_grad: float32 [32768, 1024], P(('kpt', 'row')), parts along dimension 0
There are 2 independent parts, one for each index of `kpt`. A program takes and returns all parts, laid end to end along the dimension named above; each array names one. Nothing has to cross between parts.
Inputs may be any that keep to these rules, and one draw needn't show every extreme that they name: `correlation_zero`: each correlation matrix is symmetric. `correlation_one`: each correlation matrix is symmetric.
All inputs are finite; a program needn't handle non-finite values.
Results may differ from a plain program's by a relative error of at most 0.000059.
Values sent between devices are 32-bit elements; how exact they have to be, the bound alone decides.
No kernel may reach another device: no remote copies, remote signals or barrier semaphores. Data moves between devices by JAX's collectives and lax.ppermute only.
A program may use at most 128 MiB of HBM per device.

v0:
```python
import jax
import jax.numpy as jnp
from jax import lax
from jax.sharding import PartitionSpec as P

highest = lax.Precision.HIGHEST


def back_step(orbitals, correlation, incoming):
    direct_term = 1.5 * incoming - 0.5 * jnp.dot(
        incoming, correlation, precision=highest, preferred_element_type=jnp.float32
    )
    local_gram = lax.dot_general(
        orbitals,
        incoming,
        (((0,), (0,)), ((), ())),
        precision=highest,
        preferred_element_type=jnp.float32,
    )
    gram_total = lax.psum(local_gram, "row")
    symmetric = gram_total + gram_total.T
    mixed = jnp.dot(orbitals, symmetric, precision=highest, preferred_element_type=jnp.float32)
    return direct_term - 0.5 * mixed


def body(orbitals_zero, orbitals_one, correlation_zero, correlation_one, cotangent):
    middle = back_step(orbitals_one, correlation_one, cotangent)
    return back_step(orbitals_zero, correlation_zero, middle)


def solution(mesh):
    in_specs = (
        P(("kpt", "row"), None),
        P(("kpt", "row"), None),
        P("kpt", None),
        P("kpt", None),
        P(("kpt", "row"), None),
    )
    out_specs = P(("kpt", "row"), None)
    return jax.shard_map(body, mesh=mesh, in_specs=in_specs, out_specs=out_specs, check_vma=False)
```

profile of v0, /device:TPU:0, one launch (start us, length us, event | category | flops | bytes accessed | tf_op | source)
XLA Modules:
  0.0 323.0 jit_solution(5459739876822404836)
XLA Ops:
  6.5 0.0 all-reduce.3.cloned.1.call-start
  6.5 17.6 %fusion.3 = f32[1024,1024]{1,0:T(8,128)} fusion(f32[1024,1024]{1,0:T(8,128)} %param.6, f32[1024,1024]{1,0:T(8,128)} %param.9), kind=kOutput, calls=%fused_computation.9 | convolution fusion | flops 12884901888 | bytes 12582912 | tf_op jit(solution)/shard_map/dot_general | solution.py:13
  24.1 0.0 all-reduce.3.cloned.1.call-update
  24.1 0.2 all-reduce.5.cloned.1.call-start
  24.4 17.5 %fusion.2 = f32[1024,1024]{1,0:T(8,128)} fusion(f32[1024,1024]{1,0:T(8,128)} %param.9, f32[1024,1024]{1,0:T(8,128)} %param.8), kind=kOutput, calls=%fused_computation.8 | convolution fusion | flops 12884901888 | bytes 12582912 | tf_op jit(solution)/shard_map/dot_general | solution.py:10
  41.9 96.6 %all-reduce.3.cloned.1.call-done = f32[1024,1024]{1,0:T(8,128)} async-done(((f32[1024,1024]{1,0:T(8,128)}), f32[1024,1024]{1,0:T(8,128)}) %all-reduce.3.cloned.1.call-update) | async-done | bytes 4194320 | tf_op jit(solution)/shard_map/psum | solution.py:20
  138.5 5.4 %copy.7 = f32[1024,1024]{0,1:T(8,128)} copy(f32[1024,1024]{1,0:T(8,128)} %all-reduce.3.cloned.1.call-done) | data formatting | bytes 8388608 | tf_op jit(solution)/shard_map/psum | solution.py:20
  143.9 0.0 copy-start.1
  143.9 20.3 %bitcast_subtract_fusion.1 = f32[1024,1024]{1,0:T(8,128)S(1)} fusion(f32[1024,1024]{1,0:T(8,128)} %fusion.2, f32[1024,1024]{1,0:T(8,128)} %param.9, f32[1024,1024]{1,0:T(8,128)} %param.6, f32[1024,1024]{1,0:T(8,128)} %all-reduce.3.cloned.1.call-done, f32[1024,1024]{0,1:T(8,128)} %copy.7), kind=kOutput, calls=%fused_computation.3 | convolution fusion | flops 12891193344 | bytes 25165824 | tf_op jit(solution)/shard_map/dot_general | solution.py:22
  164.2 0.0 copy-start
  164.2 2.0 copy-done
  166.2 0.0 copy-done.1
  166.2 15.0 %convolution_bitcast_fusion = f32[1024,1024]{0,1:T(8,128)} fusion(f32[1024,1024]{1,0:T(8,128)S(1)} %bitcast_subtract_fusion.1, f32[1024,1024]{1,0:T(8,128)S(1)} %copy-done.1), kind=kOutput, calls=%fused_computation.6 | convolution fusion | flops 12884901888 | bytes 12582912 | tf_op jit(solution)/shard_map/dot_general | solution.py:13
  181.1 0.0 all-reduce.5.cloned.1.call-update
  181.2 18.0 %convolution_multiply_fusion = f32[1024,1024]{0,1:T(8,128)} fusion(f32[1024,1024]{1,0:T(8,128)} %copy-done, f32[1024,1024]{1,0:T(8,128)} %param.7), kind=kOutput, calls=%fused_computation.7 | convolution fusion | flops 12885950464 | bytes 12582912 | tf_op jit(solution)/shard_map/dot_general | solution.py:10
  199.2 5.4 %copy.10 = f32[1024,1024]{1,0:T(8,128)} copy(f32[1024,1024]{0,1:T(8,128)} %convolution_multiply_fusion) | data formatting | bytes 8388608 | tf_op jit(solution)/shard_map/mul | solution.py:10
  204.6 87.2 %all-reduce.5.cloned.1.call-done = f32[1024,1024]{0,1:T(8,128)} async-done(((f32[1024,1024]{0,1:T(8,128)}), f32[1024,1024]{0,1:T(8,128)}) %all-reduce.5.cloned.1.call-update) | async-done | bytes 4194320 | tf_op jit(solution)/shard_map/psum | solution.py:20
  291.8 5.3 %copy.11 = f32[1024,1024]{1,0:T(8,128)} copy(f32[1024,1024]{0,1:T(8,128)} %all-reduce.5.cloned.1.call-done) | data formatting | bytes 8388608 | tf_op jit(solution)/shard_map/psum | solution.py:20
  297.1 19.0 %bitcast_subtract_fusion = f32[1024,1024]{1,0:T(8,128)} fusion(f32[1024,1024]{1,0:T(8,128)} %copy.10, f32[1024,1024]{1,0:T(8,128)} %copy-done, f32[1024,1024]{1,0:T(8,128)} %param.5, f32[1024,1024]{0,1:T(8,128)} %all-reduce.5.cloned.1.call-done, f32[1024,1024]{1,0:T(8,128)} %copy.11), kind=kOutput, calls=%fused_computation | convolution fusion | flops 12890144768 | bytes 25165824 | tf_op jit(solution)/shard_map/dot_general | solution.py:22
Async XLA Ops:
  6.5 132.0 %all-reduce.3.cloned.1.call-start = ((), (), s32[]{:S(2)}) async-start(), calls=%async_computation | async-start | bytes 8388608 | tf_op jit(solution)/shard_map/psum | solution.py:20
  24.1 267.6 %all-reduce.5.cloned.1.call-start = ((), (), s32[]{:S(2)}) async-start(), calls=%async_computation.1 | async-start | bytes 8388608 | tf_op jit(solution)/shard_map/psum | solution.py:20
  143.9 22.3 %copy-start.1 = (f32[1024,1024]{1,0:T(8,128)S(1)}, f32[1024,1024]{1,0:T(8,128)}, u32[]{:S(2)}) copy-start(f32[1024,1024]{1,0:T(8,128)} %param.5) | copy-start | bytes 12582916
  164.2 2.0 copy-start
Sparse Core Ops, SparseCore 0:
  24.3 114.1 all-reduce.2
  181.3 110.4 all-reduce.4
where the time goes:
time: 323 us
  waiting for transfers between devices  184 us (57%)
  matrix products  107 us (33%)
  local copies, waits for them, and re-layouts  18.1 us (6%)
  between operations  13.4 us (4%)
    psum x2, waiting for transfers between devices, back_step(): gram_total = lax.psum(local_gram, 'row')  184 us
    dot_general x2, matrix products, back_step(): jnp.dot(orbitals, symmetric, precision=highest, preferred_element_type=jn...  39.3 us
    dot_general x2, matrix products, back_step(): jnp.dot(incoming, correlation, precision=highest, preferred_element_type=...  35.5 us
    dot_general x2, matrix products, back_step(): lax.dot_general(orbitals, incoming, (((0,), (0,)), ((), ())), precision=h...  32.5 us
    psum x2, local copies, waits for them, and re-layouts, back_step(): gram_total = lax.psum(local_gram, 'row')  10.7 us
  transfers between devices with their start and end apart: 2, of which 2 were waited for; matrix products, arithmetic and copies ran while one was open for 13% of the time, Pallas kernels for 0%

commit v1 on v0

v1 whole, which is shorter than its diff:
```python
import jax
import jax.numpy as jnp
from jax import lax
from jax.sharding import PartitionSpec as P

HIGH = lax.Precision.HIGH
B = 128


def mm(a, b):
    return jnp.dot(a, b, precision=HIGH, preferred_element_type=jnp.float32)


def mm_t(a, b):
    return lax.dot_general(
        a, b, (((0,), (0,)), ((), ())), precision=HIGH, preferred_element_type=jnp.float32
    )


def pack(sym):
    n = sym.shape[0] // B
    rows = [sym[i * B:(i + 1) * B, i * B:] for i in range(n)]
    return jnp.concatenate(
        [jnp.concatenate([rows[i], rows[n - 1 - i]], axis=1) for i in range(n // 2)], axis=0
    )


def unpack(packed):
    n = 2 * packed.shape[0] // B
    rows = [None] * n
    for i in range(n // 2):
        line = packed[i * B:(i + 1) * B]
        rows[i] = line[:, :(n - i) * B]
        rows[n - 1 - i] = line[:, (n - i) * B:]
    full = []
    for i in range(n):
        left = [rows[j][:, (i - j) * B:(i - j + 1) * B].T for j in range(i)]
        full.append(jnp.concatenate(left + [rows[i]], axis=1))
    return jnp.concatenate(full, axis=0)


def back_step(orbitals, correlation, incoming):
    gram = mm_t(orbitals, incoming)
    total = lax.psum(pack(gram + gram.T), "row")
    direct = 1.5 * incoming - 0.5 * mm(incoming, correlation)
    return direct - 0.5 * mm(orbitals, unpack(total))


def body(orbitals_zero, orbitals_one, correlation_zero, correlation_one, cotangent):
    middle = back_step(orbitals_one, correlation_one, cotangent)
    return back_step(orbitals_zero, correlation_zero, middle)


def solution(mesh):
    in_specs = (
        P(("kpt", "row"), None),
        P(("kpt", "row"), None),
        P("kpt", None),
        P("kpt", None),
        P(("kpt", "row"), None),
    )
    out_specs = P(("kpt", "row"), None)
    return jax.shard_map(body, mesh=mesh, in_specs=in_specs, out_specs=out_specs, check_vma=False)
```

time: 323 us -> 329 us (1.019)
  local copies, waits for them, and re-layouts: 18.1 us -> 66.8 us
  matrix products: 107 us -> 61.6 us
  other arithmetic: 0 us -> 12.3 us
  waiting for transfers between devices: 184 us -> 173 us
    dot_general x6, matrix products: 107 us -> 61.6 us  [the longest x4 42.1 us: mm(): return jnp.dot(a, b, precision=HIGH, preferred_element_type=jnp.float32)]
    unnamed x4 -> x180, local copies, waits for them, and re-layouts: 2.01 us -> 43.2 us
    psum x2, waiting for transfers between devices: 184 us -> 173 us  [back_step(): total = lax.psum(pack(gram + gram.T), 'row')]
    dot_general x0 -> x2, local copies, waits for them, and re-layouts: none -> 10.8 us  [mm_t(): lax.dot_general(a, b, (((0,), (0,)), ((), ())), precision=HIGH, preferred...]
    psum x2 -> x0, local copies, waits for them, and re-layouts: 10.7 us -> none  [back_step(): gram_total = lax.psum(local_gram, 'row')]
    add x0 -> x2, other arithmetic: none -> 8.79 us  [back_step(): total = lax.psum(pack(gram + gram.T), 'row')]
    slice x0 -> x26, local copies, waits for them, and re-layouts: none -> 7.35 us  [the longest x4 6.82 us: unpack(): left = [rows[j][:, (i - j) * B:(i - j + 1) * B].T for j in range(i)]]
  transfers between devices with their start and end apart: 2 -> 2, of which waited for: 2 -> 2; matrix products, arithmetic and copies ran while one was open for 13% -> 8% of each run, Pallas kernels for 0% -> 0%
where the time goes in v1:
time: 329 us; the launch traced here: 328 us
  waiting for transfers between devices  173 us (53%)
  local copies, waits for them, and re-layouts  66.8 us (20%)
  matrix products  61.6 us (19%)
  between operations  14.5 us (4%)
  other arithmetic  12.3 us (4%)
    psum x2, waiting for transfers between devices, back_step(): total = lax.psum(pack(gram + gram.T), 'row')  173 us
    unnamed x180, local copies, waits for them, and re-layouts  43.2 us
    dot_general x4, matrix products, mm(): return jnp.dot(a, b, precision=HIGH, preferred_element_type=jnp.float32)  42.1 us
    dot_general x2, matrix products, mm_t(): lax.dot_general(a, b, (((0,), (0,)), ((), ())), precision=HIGH, preferred...  19.5 us
    dot_general x2, local copies, waits for them, and re-layouts, mm_t(): lax.dot_general(a, b, (((0,), (0,)), ((), ())), precision=HIGH, preferred...  10.8 us
    add x2, other arithmetic, back_step(): total = lax.psum(pack(gram + gram.T), 'row')  8.79 us
    slice x4, local copies, waits for them, and re-layouts, unpack(): left = [rows[j][:, (i - j) * B:(i - j + 1) * B].T for j in range(i)]  6.82 us
  transfers between devices with their start and end apart: 2, of which 2 were waited for; matrix products, arithmetic and copies ran while one was open for 8% of the time, Pallas kernels for 0%

profile of v1, /device:TPU:0, one launch (start us, length us, event | category | flops | bytes accessed | tf_op | source)
XLA Modules:
  0.0 328.1 jit_solution(12613404270405732038)
XLA Ops:
  6.5 11.1 %fusion.5 = f32[1024,1024]{1,0:T(8,128)} fusion(f32[1024,1024]{1,0:T(8,128)} %param.6, f32[1024,1024]{1,0:T(8,128)} %param.9), kind=kOutput, calls=%fused_computation.72 | convolution fusion | flops 6442450944 | bytes 12582912 | tf_op jit(solution)/shard_map/dot_general | solution.py:15
  17.6 5.4 %copy.7 = f32[1024,1024]{0,1:T(8,128)} copy(f32[1024,1024]{1,0:T(8,128)} %fusion.5) | data formatting | bytes 8388608 | tf_op jit(solution)/shard_map/dot_general | solution.py:15
  23.0 4.4 %bitcast_add_fusion.1 = f32[1024,1024]{1,0:T(8,128)S(1)} fusion(f32[1024,1024]{1,0:T(8,128)} %fusion.5, f32[1024,1024]{0,1:T(8,128)} %copy.7), kind=kLoop, calls=%fused_computation.3 | loop fusion | flops 1048576 | bytes 12582912 | tf_op jit(solution)/shard_map/add | solution.py:44
  27.6 1.6 maximum_maximum_fusion
  29.5 11.0 %fusion.4 = f32[1024,1024]{1,0:T(8,128)} fusion(f32[1024,1024]{1,0:T(8,128)} %param.9, f32[1024,1024]{1,0:T(8,128)} %param.8), kind=kOutput, calls=%fused_computation.71 | convolution fusion | flops 6442450944 | bytes 12582912 | tf_op jit(solution)/shard_map/dot_general | solution.py:11
  40.5 90.8 %all-reduce.3.cloned.1.call-done = f32[512,1152]{1,0:T(8,128)} async-done(((f32[512,1152]{1,0:T(8,128)}), f32[512,1152]{1,0:T(8,128)}) %all-reduce.3.cloned.1.call-update) | async-done | bytes 2359312 | tf_op jit(solution)/shard_map/psum | solution.py:44
  135.4 2.1 fusion.2
  137.6 1.6 copy.81
  139.1 1.6 copy.82
  140.7 1.6 copy.83
  142.3 1.6 copy.84
  143.8 1.6 copy.85
  145.4 1.6 copy.86
  147.0 1.6 copy.87
  156.0 9.5 %bitcast_subtract_fusion.1 = f32[1024,1024]{1,0:T(8,128)S(1)} fusion(f32[1024,1024]{1,0:T(8,128)} %fusion.4, f32[1024,1024]{1,0:T(8,128)S(1)} %copy-done.5, f32[1024,1024]{1,0:T(8,128)S(1)} %slice_dynamic-update-slice_fusion.9, f32[1024,1024]{1,0:T(8,128)S(1)} %copy-done.6), kind=kOutput, calls=%fused_computation.2 | convolution fusion | flops 6447693824 | bytes 20971520 | tf_op jit(solution)/shard_map/dot_general | solution.py:11
  165.6 2.0 copy-done
  167.6 8.5 %fusion.6 = f32[1024,1024]{1,0:T(8,128)} fusion(f32[1024,1024]{1,0:T(8,128)S(1)} %bitcast_subtract_fusion.1, f32[1024,1024]{1,0:T(8,128)S(1)} %copy-done.7), kind=kOutput, calls=%fused_computation.73 | convolution fusion | flops 6442450944 | bytes 12582912 | tf_op jit(solution)/shard_map/dot_general | solution.py:15
  176.0 5.4 %copy.39 = f32[1024,1024]{0,1:T(8,128)} copy(f32[1024,1024]{1,0:T(8,128)} %fusion.6) | data formatting | bytes 8388608 | tf_op jit(solution)/shard_map/dot_general | solution.py:15
  181.5 4.4 %bitcast_add_fusion = f32[1024,1024]{1,0:T(8,128)S(1)} fusion(f32[1024,1024]{1,0:T(8,128)} %fusion.6, f32[1024,1024]{0,1:T(8,128)} %copy.39), kind=kLoop, calls=%fused_computation.1 | loop fusion | flops 1048576 | bytes 12582912 | tf_op jit(solution)/shard_map/add | solution.py:44
  186.1 1.7 maximum_maximum_fusion.1
  187.8 11.2 %convolution_multiply_fusion = f32[1024,1024]{0,1:T(8,128)} fusion(f32[1024,1024]{1,0:T(8,128)} %copy-done, f32[1024,1024]{1,0:T(8,128)} %param.7), kind=kOutput, calls=%fused_computation.6 | convolution fusion | flops 6443499520 | bytes 12582912 | tf_op jit(solution)/shard_map/dot_general | solution.py:11
  199.0 5.4 %copy.38 = f32[1024,1024]{1,0:T(8,128)} copy(f32[1024,1024]{0,1:T(8,128)} %convolution_multiply_fusion) | data formatting | bytes 8388608 | tf_op jit(solution)/shard_map/mul | solution.py:45
  204.4 81.8 %all-reduce.5.cloned.1.call-done = f32[512,1152]{1,0:T(8,128)} async-done(((f32[512,1152]{1,0:T(8,128)}), f32[512,1152]{1,0:T(8,128)}) %all-reduce.5.cloned.1.call-update) | async-done | bytes 2359312 | tf_op jit(solution)/shard_map/psum | solution.py:44
  290.3 2.1 fusion
  292.4 1.6 copy.109
  293.9 1.6 copy.110
  295.5 1.6 copy.111
  297.1 1.6 copy.112
  298.6 1.6 copy.113
  300.2 1.6 copy.114
  301.8 1.6 copy.115
  310.9 10.4 %bitcast_subtract_fusion = f32[1024,1024]{1,0:T(8,128)} fusion(f32[1024,1024]{1,0:T(8,128)S(1)} %copy-done.2, f32[1024,1024]{1,0:T(8,128)S(1)} %copy-done.1, f32[1024,1024]{1,0:T(8,128)S(1)} %slice_dynamic-update-slice_fusion.8, f32[1024,1024]{1,0:T(8,128)} %param.5), kind=kOutput, calls=%fused_computation | convolution fusion | flops 6446645248 | bytes 20971520 | tf_op jit(solution)/shard_map/dot_general | solution.py:11
  (201 shorter events, 22.9 us)
Async XLA Ops:
  6.5 124.8 %all-reduce.3.cloned.1.call-start = ((), (), s32[]{:S(2)}) async-start(), calls=%async_computation | async-start | bytes 4718592 | tf_op jit(solution)/shard_map/psum | solution.py:44
  29.3 256.9 %all-reduce.5.cloned.1.call-start = ((), (), s32[]{:S(2)}) async-start(), calls=%async_computation.1 | async-start | bytes 4718592 | tf_op jit(solution)/shard_map/psum | solution.py:44
  131.3 20.9 %copy-start.3 = (f32[512,1152]{1,0:T(8,128)S(1)}, f32[512,1152]{1,0:T(8,128)}, u32[]{:S(2)}) copy-start(f32[512,1152]{1,0:T(8,128)} %all-reduce.3.cloned.1.call-done) | copy-start | bytes 7077892
  149.2 3.4 %copy-start.8 = (f32[128,128]{0,1:T(8,128)S(1)}, f32[128,128]{0,1:T(8,128)}, u32[]{:S(2)}) copy-start(f32[128,128]{0,1:T(8,128)} %copy.79) | copy-start | bytes 196612
  150.0 2.7 copy-start.9
  150.7 2.0 copy-start.12
  152.2 0.9 copy-start.28
  152.3 0.9 copy-start.26
  152.3 1.0 copy-start.24
  152.3 1.0 copy-start.22
  152.3 1.0 copy-start.20
  152.3 1.0 copy-start.18
  152.4 1.0 copy-start.16
  152.4 1.0 copy-start.14
  152.4 2.4 copy-start.5
  152.4 3.6 %copy-start.6 = (f32[1024,1024]{1,0:T(8,128)S(1)}, f32[1024,1024]{1,0:T(8,128)}, u32[]{:S(2)}) copy-start(f32[1024,1024]{1,0:T(8,128)} %param.6) | copy-start | bytes 12582916
  156.0 11.5 %copy-start.7 = (f32[1024,1024]{1,0:T(8,128)S(1)}, f32[1024,1024]{1,0:T(8,128)}, u32[]{:S(2)}) copy-start(f32[1024,1024]{1,0:T(8,128)} %param.5) | copy-start | bytes 12582916
  165.5 2.0 copy-start
  286.2 20.9 %copy-start.4 = (f32[512,1152]{1,0:T(8,128)S(1)}, f32[512,1152]{1,0:T(8,128)}, u32[]{:S(2)}) copy-start(f32[512,1152]{1,0:T(8,128)} %all-reduce.5.cloned.1.call-done) | copy-start | bytes 7077892
  304.1 3.5 %copy-start.10 = (f32[128,128]{0,1:T(8,128)S(1)}, f32[128,128]{0,1:T(8,128)}, u32[]{:S(2)}) copy-start(f32[128,128]{0,1:T(8,128)} %copy.107) | copy-start | bytes 196612
  304.8 2.8 copy-start.11
  305.5 2.0 copy-start.13
  307.1 0.9 copy-start.29
  307.1 0.9 copy-start.27
  307.1 1.0 copy-start.25
  307.1 1.0 copy-start.23
  307.1 1.0 copy-start.21
  307.2 1.0 copy-start.19
  307.2 1.0 copy-start.17
  307.2 1.0 copy-start.15
  307.3 2.4 copy-start.1
  307.3 3.6 %copy-start.2 = (f32[1024,1024]{1,0:T(8,128)S(1)}, f32[1024,1024]{1,0:T(8,128)}, u32[]{:S(2)}) copy-start(f32[1024,1024]{1,0:T(8,128)} %copy.38) | copy-start | bytes 12582916
  (6 other events, 5.2 us)
Sparse Core Ops, SparseCore 0:
  29.4 101.9 all-reduce.2
  187.9 98.1 all-reduce.4

commit v2 on v0

v2 whole, which is shorter than its diff:
```python
import functools
import jax
import jax.numpy as jnp
from jax import lax
from jax.experimental import pallas as pl
from jax.experimental.pallas import tpu as pltpu
from jax.sharding import PartitionSpec as P

F32 = jnp.float32
BF16 = jnp.bfloat16
B = 128
TILE = 256
LIMIT = 44 * 1024 * 1024


def split(x):
    hi = x.astype(BF16)
    return hi, (x - hi.astype(F32)).astype(BF16)


def dot3(a, b, dims):
    (ah, al), (bh, bl) = a, b
    one = lambda p, q: lax.dot_general(p, q, (dims, ((), ())), preferred_element_type=F32)
    return one(ah, bh) + (one(ah, bl) + one(al, bh))


NN = ((1,), (0,))
TN = ((0,), (0,))


def params(**kw):
    return pltpu.CompilerParams(vmem_limit_bytes=LIMIT, **kw)


def cost(products, size, arrays):
    return pl.CostEstimate(
        flops=6 * products * size ** 3, bytes_accessed=4 * arrays * size * size, transcendentals=0
    )


def pack_into(g, packed, me, shards):
    size = g.shape[0]
    n = size // B
    rows = size // 2 // shards
    for i in range(n // 2):
        at = 0
        for top in (i, n - 1 - i):
            for j in range(top, n):
                p = slice(top * B, (top + 1) * B)
                q = slice(j * B, (j + 1) * B)
                block = g[p, q] + g[q, p].T
                for s in range(B // rows):
                    slot = (i * (B // rows) + s) ^ me
                    packed[pl.ds(pl.multiple_of(slot * rows, rows), rows), at:at + B] = (
                        block[s * rows:(s + 1) * rows]
                    )
                at += B


def unpack_into(pieces, packed, hi, lo, me, shards):
    size = hi.shape[0]
    n = size // B
    rows = size // 2 // shards
    slot = 0
    for piece in pieces:
        for s in range(piece.shape[0] // rows):
            at = pl.multiple_of((slot ^ me) * rows, rows)
            packed[pl.ds(at, rows), :] = piece[s * rows:(s + 1) * rows, :]
            slot += 1
    for i in range(n // 2):
        at = 0
        for top in (i, n - 1 - i):
            for j in range(top, n):
                p = slice(top * B, (top + 1) * B)
                q = slice(j * B, (j + 1) * B)
                block = packed[i * B:(i + 1) * B, at:at + B]
                hi[p, q], lo[p, q] = split(block)
                if j > top:
                    hi[q, p], lo[q, p] = split(block.T)
                at += B


def gram_kernel(a_ref, b_ref, out_ref):
    @pl.when(pl.program_id(0) == 0)
    def _():
        out_ref[...] = jnp.zeros_like(out_ref)

    out_ref[...] += dot3(split(a_ref[...]), split(b_ref[...]), TN)


def gram(a, b):
    rows, size = a.shape
    block = pl.BlockSpec((TILE, size), lambda r: (r, 0))
    return pl.pallas_call(
        gram_kernel,
        grid=(rows // TILE,),
        in_specs=[block, block],
        out_specs=pl.BlockSpec((size, size), lambda r: (0, 0)),
        out_shape=jax.ShapeDtypeStruct((size, size), F32),
        compiler_params=params(),
        cost_estimate=cost(1, size, 3),
    )(a, b)


def gram_pack_kernel(shards, me_ref, a_ref, b_ref, keep_ref, send_ref, g, packed):
    step = pl.program_id(0)

    @pl.when(step == 0)
    def _():
        g[...] = jnp.zeros_like(g)

    g[...] += dot3(split(a_ref[...]), split(b_ref[...]), TN)

    @pl.when(step == pl.num_programs(0) - 1)
    def _():
        pack_into(g, packed, me_ref[0], shards)
        half = keep_ref.shape[0]
        keep_ref[...] = packed[:half]
        send_ref[...] = packed[half:]


def packed_shape(size):
    return size // 2, size + B


def gram_pack(me, shards, a, b):
    rows, size = a.shape
    height, width = packed_shape(size)
    block = pl.BlockSpec((TILE, size), lambda r: (r, 0))
    half = pl.BlockSpec((height // 2, width), lambda r: (0, 0))
    return pl.pallas_call(
        functools.partial(gram_pack_kernel, shards),
        grid=(rows // TILE,),
        in_specs=[pl.BlockSpec(memory_space=pltpu.SMEM), block, block],
        out_specs=[half, half],
        out_shape=[jax.ShapeDtypeStruct((height // 2, width), F32)] * 2,
        scratch_shapes=[pltpu.VMEM((size, size), F32), pltpu.VMEM((height, width), F32)],
        compiler_params=params(),
        cost_estimate=cost(1, size, 3),
    )(me, a, b)


def affine_kernel(a_ref, b_ref, out_ref, hi, lo):
    @pl.when(pl.program_id(0) == 0)
    def _():
        hi[...], lo[...] = split(b_ref[...])

    a = a_ref[...]
    out_ref[...] = 1.5 * a - 0.5 * dot3(split(a), (hi[...], lo[...]), NN)


def affine(a, b):
    rows, size = a.shape
    block = pl.BlockSpec((TILE, size), lambda r: (r, 0))
    return pl.pallas_call(
        affine_kernel,
        grid=(rows // TILE,),
        in_specs=[block, pl.BlockSpec((size, size), lambda r: (0, 0))],
        out_specs=block,
        out_shape=jax.ShapeDtypeStruct((rows, size), F32),
        scratch_shapes=[pltpu.VMEM((size, size), BF16)] * 2,
        compiler_params=params(),
        cost_estimate=cost(1, size, 3),
    )(a, b)


def second_gram_kernel(shards, count, me_ref, *refs):
    pieces = refs[:count]
    w_ref, p_ref, hi, lo, keep_ref, send_ref, g, packed = refs[count:]
    step = pl.program_id(0)

    @pl.when(step == 0)
    def _():
        unpack_into(pieces, packed, hi, lo, me_ref[0], shards)

    tile = w_ref.shape[0]
    at = pl.multiple_of(step * tile, tile)
    g[pl.ds(at, tile), :] = p_ref[...] - 0.5 * dot3(split(w_ref[...]), (hi[...], lo[...]), NN)

    @pl.when(step == pl.num_programs(0) - 1)
    def _():
        pack_into(g, packed, me_ref[0], shards)
        half = keep_ref.shape[0]
        keep_ref[...] = packed[:half]
        send_ref[...] = packed[half:]


def second_gram(me, shards, pieces, w, p):
    size = w.shape[0]
    height, width = packed_shape(size)
    block = pl.BlockSpec((TILE, size), lambda r: (r, 0))
    whole = lambda x: pl.BlockSpec(x, lambda r: (0, 0))
    return pl.pallas_call(
        functools.partial(second_gram_kernel, shards, len(pieces)),
        grid=(size // TILE,),
        in_specs=[pl.BlockSpec(memory_space=pltpu.SMEM)]
        + [whole(x.shape) for x in pieces]
        + [block, block],
        out_specs=[whole((size, size))] * 2 + [whole((height // 2, width))] * 2,
        out_shape=[jax.ShapeDtypeStruct((size, size), BF16)] * 2
        + [jax.ShapeDtypeStruct((height // 2, width), F32)] * 2,
        scratch_shapes=[pltpu.VMEM((size, size), F32), pltpu.VMEM((height, width), F32)],
        compiler_params=params(),
        cost_estimate=cost(1, size, 5),
    )(me, *pieces, w, p)


def middle_kernel(x_ref, hi_ref, lo_ref, m_ref, s_ref, out_ref, sh, sl):
    @pl.when(pl.program_id(0) == 0)
    def _():
        sh[...], sl[...] = split(s_ref[...])

    mid = m_ref[...] - 0.5 * dot3(split(x_ref[...]), (hi_ref[...], lo_ref[...]), NN)
    out_ref[...] = 1.5 * mid - 0.5 * dot3(split(mid), (sh[...], sl[...]), NN)


def middle_affine(x, hi, lo, m, s):
    rows, size = x.shape
    block = pl.BlockSpec((TILE, size), lambda r: (r, 0))
    whole = pl.BlockSpec((size, size), lambda r: (0, 0))
    return pl.pallas_call(
        middle_kernel,
        grid=(rows // TILE,),
        in_specs=[block, whole, whole, block, whole],
        out_specs=block,
        out_shape=jax.ShapeDtypeStruct((rows, size), F32),
        scratch_shapes=[pltpu.VMEM((size, size), BF16)] * 2,
        compiler_params=params(),
        cost_estimate=cost(2, size, 5),
    )(x, hi, lo, m, s)


def last_kernel(shards, count, me_ref, *refs):
    pieces = refs[:count]
    x_ref, d_ref, out_ref, hi, lo, packed = refs[count:]

    @pl.when(pl.program_id(0) == 0)
    def _():
        unpack_into(pieces, packed, hi, lo, me_ref[0], shards)

    out_ref[...] = d_ref[...] - 0.5 * dot3(split(x_ref[...]), (hi[...], lo[...]), NN)


def last_step(me, shards, pieces, x, d):
    rows, size = x.shape
    block = pl.BlockSpec((TILE, size), lambda r: (r, 0))
    return pl.pallas_call(
        functools.partial(last_kernel, shards, len(pieces)),
        grid=(rows // TILE,),
        in_specs=[pl.BlockSpec(memory_space=pltpu.SMEM)]
        + [pl.BlockSpec(p.shape, lambda r: (0, 0)) for p in pieces]
        + [block, block],
        out_specs=block,
        out_shape=jax.ShapeDtypeStruct((rows, size), F32),
        scratch_shapes=[pltpu.VMEM((size, size), BF16)] * 2
        + [pltpu.VMEM(packed_shape(size), F32)],
        compiler_params=params(),
        cost_estimate=cost(1, size, 4),
    )(me, *pieces, x, d)


def stages_of(count):
    stages, stride = [], 1
    while stride < count:
        left = count // stride
        radix = 2 if stride < 4 or left % 4 else 4
        stages.append((stride, radix))
        stride *= radix
    return stages


def slot_of(index, stages):
    slot = 0
    for stride, radix in stages:
        slot = slot * radix + (index // stride) % radix
    return slot


def swap(x, offset, count):
    return lax.ppermute(x, "row", [(i, i ^ offset) for i in range(count)])


def scatter_sum(keep, send, stages, count):
    stride, radix = stages[0]
    got = [swap(send, stride, count)]
    for at, (stride, radix) in enumerate(stages):
        if at == 0:
            continue
        part = keep.shape[0] // radix
        pick = lambda k: sum((g[k * part:(k + 1) * part] for g in got), keep[k * part:(k + 1) * part])
        sends = [pick(k) for k in range(1, radix)]
        new = [swap(x, stride * (k + 1), count) for k, x in enumerate(sends)]
        keep = pick(0)
        got = new
    return sum(got, keep)


def gather(piece, stages, count):
    pieces = [piece]
    for at, (stride, radix) in reversed(list(enumerate(stages))):
        pieces = pieces + [swap(x, stride * k, count) for k in range(1, radix) for x in pieces]
        if at > 1:
            pieces = [jnp.concatenate(pieces, axis=0)]
    return pieces


def body(count, orbitals_zero, orbitals_one, correlation_zero, correlation_one, cotangent):
    stages = stages_of(count)
    me = slot_of(lax.axis_index("row"), stages).astype(jnp.int32).reshape(1)

    keep, send = gram_pack(me, count, orbitals_one, cotangent)
    direct = affine(cotangent, correlation_one)
    p = gram(orbitals_zero, direct)
    w = gram(orbitals_zero, orbitals_one)
    pieces = gather(scatter_sum(keep, send, stages, count), stages, count)

    hi, lo, keep, send = second_gram(me, count, pieces, w, p)
    direct = middle_affine(orbitals_one, hi, lo, direct, correlation_zero)
    pieces = gather(scatter_sum(keep, send, stages, count), stages, count)

    return last_step(me, count, pieces, orbitals_zero, direct)


def solution(mesh):
    in_specs = (
        P(("kpt", "row"), None),
        P(("kpt", "row"), None),
        P("kpt", None),
        P("kpt", None),
        P(("kpt", "row"), None),
    )
    out_specs = P(("kpt", "row"), None)
    return jax.shard_map(
        functools.partial(body, mesh.shape["row"]),
        mesh=mesh, in_specs=in_specs, out_specs=out_specs, check_vma=False,
    )
```

time: 323 us -> 195 us (0.60)
  matrix products: 107 us -> 0 us
  waiting for transfers between devices: 184 us -> 80.6 us
  Pallas kernels: 0 us -> 77.5 us
  starting transfers between devices: 0.22 us -> 25.5 us
  between operations: 13.4 us -> 0.14 us
  local copies, waits for them, and re-layouts: 18.1 us -> 10.1 us
    psum x2 -> x0, waiting for transfers between devices: 184 us -> none  [back_step(): gram_total = lax.psum(local_gram, 'row')]
    dot_general x6 -> x0, matrix products: 107 us -> none  [the longest x2 39.3 us: back_step(): jnp.dot(orbitals, symmetric, precision=highest, preferred_element_type=jn...]
    ppermute x0 -> x22, waiting for transfers between devices: none -> 80.6 us  [swap(): return lax.ppermute(x, 'row', [(i, i ^ offset) for i in range(count)])]
    pallas_call x0 -> x7, Pallas kernels: none -> 77.5 us  [the longest x2 18.8 us: gram(): pl.pallas_call(gram_kernel, grid=(rows // TILE,), in_specs=[block, block]...]
    ppermute x0 -> x22, starting transfers between devices: none -> 25.5 us  [swap(): return lax.ppermute(x, 'row', [(i, i ^ offset) for i in range(count)])]
    psum x2 -> x0, local copies, waits for them, and re-layouts: 10.7 us -> none  [back_step(): gram_total = lax.psum(local_gram, 'row')]
    unnamed x4 -> x14, local copies, waits for them, and re-layouts: 2.01 us -> 10.1 us
    mul x1 -> x0, local copies, waits for them, and re-layouts: 5.44 us -> none  [back_step(): 0.5 * jnp.dot(incoming, correlation, precision=highest, preferred_element...]
  transfers between devices with their start and end apart: 2 -> 22, of which waited for: 2 -> 14; matrix products, arithmetic and copies ran while one was open for 13% -> 0% of each run, Pallas kernels for 0% -> 24%
where the time goes in v2:
time: 195 us; the launch traced here: 194 us
  waiting for transfers between devices  80.6 us (41%)
  Pallas kernels  77.5 us (40%)
  starting transfers between devices  25.5 us (13%)
  local copies, waits for them, and re-layouts  10.1 us (5%)
    ppermute x22, waiting for transfers between devices, swap(): return lax.ppermute(x, 'row', [(i, i ^ offset) for i in range(count)])  80.6 us
    ppermute x22, starting transfers between devices, swap(): return lax.ppermute(x, 'row', [(i, i ^ offset) for i in range(count)])  25.5 us
    pallas_call x2, Pallas kernels, gram(): pl.pallas_call(gram_kernel, grid=(rows // TILE,), in_specs=[block, block]...  18.8 us
    pallas_call x1, Pallas kernels, middle_affine(): pl.pallas_call(middle_kernel, grid=(rows // TILE,), in_specs=[block, whol...  17.4 us
    pallas_call x1, Pallas kernels, second_gram(): pl.pallas_call(functools.partial(second_gram_kernel, shards, len(pieces))...  10.8 us
    pallas_call x1, Pallas kernels, last_step(): pl.pallas_call(functools.partial(last_kernel, shards, len(pieces)), grid=...  10.4 us
    unnamed x14, local copies, waits for them, and re-layouts  10.1 us
    pallas_call x1, Pallas kernels, affine(): pl.pallas_call(affine_kernel, grid=(rows // TILE,), in_specs=[block, pl.B...  10.1 us
  transfers between devices with their start and end apart: 22, of which 14 were waited for; matrix products, arithmetic and copies ran while one was open for 0% of the time, Pallas kernels for 24%

profile of v2, /device:TPU:0, one launch (start us, length us, event | category | flops | bytes accessed | tf_op | source)
XLA Modules:
  0.0 194.4 jit_solution(4550399335994330467)
XLA Ops:
  0.0 2.2 %copy-done.1 = f32[1024,1024]{1,0:T(8,128)S(1)} copy-done((f32[1024,1024]{1,0:T(8,128)S(1)}, f32[1024,1024]{1,0:T(8,128)}, u32[]{:S(2)}) %copy-start.1) | copy-done | bytes 4194328
  2.2 9.9 %shard_map.55 = (f32[256,1152]{1,0:T(8,128)S(1)}, f32[256,1152]{1,0:T(8,128)S(1)}) custom-call(s32[1]{0:T(128)} %bitcast.me_ref, f32[1024,1024]{1,0:T(8,128)S(1)} %copy-done.1, f32[1024,1024]{1,0:T(8,128)} %a_ref.6), custom_call_target="tpu_custom_call" | custom-call | flops 6442450944 | bytes 12582912 | tf_op jit(solution)/shard_map/pallas_call | solution.py:131
  12.6 2.5 %collective-permute-done = f32[256,1152]{1,0:T(8,128)S(1)} collective-permute-done((f32[256,1152]{1,0:T(8,128)S(1)}, f32[256,1152]{1,0:T(8,128)S(1)}, u32[]{:S(2)}, u32[]{:S(2)}) %collective-permute-start) | collective-permute-done | bytes 1179680 | tf_op jit(solution)/shard_map/ppermute | solution.py:280
  15.2 3.0 %collective-permute-start.1 = (f32[128,1152]{1,0:T(8,128)S(1)}, f32[128,1152]{1,0:T(8,128)S(1)}, u32[]{:S(2)}, u32[]{:S(2)}) collective-permute-start(f32[128,1152]{1,0:T(8,128)S(1)} %get-tuple-element.20), channel_id=1, source_target_pairs={{0,2},{1,3},{2,0},{3,1},{4,6},{5,7},{6,4},{7,5},{8,10},{9,11},{10,... | collective-permute-start | bytes 1769480 | tf_op jit(solution)/shard_map/ppermute | solution.py:280
  18.2 13.6 %collective-permute-done.1 = f32[128,1152]{1,0:T(8,128)S(1)} collective-permute-done((f32[128,1152]{1,0:T(8,128)S(1)}, f32[128,1152]{1,0:T(8,128)S(1)}, u32[]{:S(2)}, u32[]{:S(2)}) %collective-permute-start.1) | collective-permute-done | bytes 589856 | tf_op jit(solution)/shard_map/ppermute | solution.py:280
  31.8 1.9 collective-permute-start.2
  33.7 2.5 %collective-permute-start.4 = (f32[32,1152]{1,0:T(8,128)S(1)}, f32[32,1152]{1,0:T(8,128)S(1)}, u32[]{:S(2)}, u32[]{:S(2)}) collective-permute-start(f32[32,1152]{1,0:T(8,128)S(1)} %get-tuple-element.25), channel_id=1, source_target_pairs={{0,12},{1,13},{2,14},{3,15},{4,8},{5,9},{6,10},{7,11},{8,4},{9,5},... | collective-permute-start | bytes 442376 | tf_op jit(solution)/shard_map/ppermute | solution.py:280
  37.5 6.5 %collective-permute-done.4 = f32[32,1152]{1,0:T(8,128)S(1)} collective-permute-done((f32[32,1152]{1,0:T(8,128)S(1)}, f32[32,1152]{1,0:T(8,128)S(1)}, u32[]{:S(2)}, u32[]{:S(2)}) %collective-permute-start.4) | collective-permute-done | bytes 147488 | tf_op jit(solution)/shard_map/ppermute | solution.py:280
  44.0 4.9 %collective-permute-done.3 = f32[32,1152]{1,0:T(8,128)S(1)} collective-permute-done((f32[32,1152]{1,0:T(8,128)S(1)}, f32[32,1152]{1,0:T(8,128)S(1)}, u32[]{:S(2)}, u32[]{:S(2)}) %collective-permute-start.3) | collective-permute-done | bytes 147488 | tf_op jit(solution)/shard_map/ppermute | solution.py:280
  48.9 3.4 %collective-permute-start.7 = (f32[32,1152]{1,0:T(8,128)S(1)}, f32[32,1152]{1,0:T(8,128)S(1)}, u32[]{:S(2)}, u32[]{:S(2)}) collective-permute-start(f32[32,1152]{1,0:T(8,128)S(1)} %fusion.5), channel_id=1, source_target_pairs={{0,12},{1,13},{2,14},{3,15},{4,8},{5,9},{6,10},{7,11},{8,4},{9,5},... | collective-permute-start | bytes 442376 | tf_op jit(solution)/shard_map/ppermute | solution.py:280
  53.3 10.1 %shard_map.57.b_ref.m_ref = f32[1024,1024]{1,0:T(8,128)S(1)} custom-call(f32[1024,1024]{1,0:T(8,128)S(1)} %copy-done, f32[1024,1024]{1,0:T(8,128)} %b_ref.5), custom_call_target="tpu_custom_call" | custom-call | flops 6442450944 | bytes 12582912 | tf_op jit(solution)/shard_map/pallas_call | solution.py:155
  63.5 1.9 %copy-done.4 = f32[1024,1024]{1,0:T(8,128)} copy-done((f32[1024,1024]{1,0:T(8,128)}, f32[1024,1024]{1,0:T(8,128)S(1)}, u32[]{:S(2)}) %copy-start.4) | copy-done | bytes 4194328
  65.5 1.6 collective-permute-start.8
  67.1 9.4 %shard_map.56.refs_4_ = f32[1024,1024]{1,0:T(8,128)S(1)} custom-call(f32[1024,1024]{1,0:T(8,128)S(1)} %copy-done.2, f32[1024,1024]{1,0:T(8,128)} %x_ref.1), custom_call_target="tpu_custom_call" | custom-call | flops 6442450944 | bytes 12582912 | tf_op jit(solution)/shard_map/pallas_call | solution.py:94
  76.5 2.0 %copy-done.5 = f32[1024,1024]{1,0:T(8,128)} copy-done((f32[1024,1024]{1,0:T(8,128)}, f32[1024,1024]{1,0:T(8,128)S(1)}, u32[]{:S(2)}) %copy-start.5) | copy-done | bytes 4194328
  79.0 9.4 %shard_map.58.refs_5_ = f32[1024,1024]{1,0:T(8,128)S(1)} custom-call(f32[1024,1024]{1,0:T(8,128)S(1)} %copy-done.2, f32[1024,1024]{1,0:T(8,128)} %copy-done.4), custom_call_target="tpu_custom_call" | custom-call | flops 6442450944 | bytes 12582912 | tf_op jit(solution)/shard_map/pallas_call | solution.py:94
  88.4 2.0 %copy-done.6 = f32[1024,1024]{1,0:T(8,128)} copy-done((f32[1024,1024]{1,0:T(8,128)}, f32[1024,1024]{1,0:T(8,128)S(1)}, u32[]{:S(2)}) %copy-start.6) | copy-done | bytes 4194328
  90.4 10.8 %shard_map.59 = (bf16[1024,1024]{1,0:T(8,128)(2,1)S(1)}, bf16[1024,1024]{1,0:T(8,128)(2,1)S(1)}, f32[256,1152]{1,0:T(8,128)S(1)}, f32[256,1152]{1,0:T(8,128)S(1)}) custom-call(s32[1]{0:T(128)} %bitcast.me_ref, f32[128,1152]{1,0:T(8,128)S(1)} %pad_maximum_fusion.refs_0_, f32[128,1152]{1,0:T(8,128)S(1)} %collective-permute-done.8.refs_1_, ...), custom_call_target="tpu_custom_call" | custom-call | flops 6442450944 | bytes 20971520 | tf_op jit(solution)/shard_map/pallas_call | solution.py:193
  101.5 2.7 %collective-permute-done.11 = f32[256,1152]{1,0:T(8,128)S(1)} collective-permute-done((f32[256,1152]{1,0:T(8,128)S(1)}, f32[256,1152]{1,0:T(8,128)S(1)}, u32[]{:S(2)}, u32[]{:S(2)}) %collective-permute-start.11) | collective-permute-done | bytes 1179680 | tf_op jit(solution)/shard_map/ppermute | solution.py:280
  104.3 1.4 collective-permute-start.12
  105.7 14.1 %collective-permute-done.12 = f32[128,1152]{1,0:T(8,128)S(1)} collective-permute-done((f32[128,1152]{1,0:T(8,128)S(1)}, f32[128,1152]{1,0:T(8,128)S(1)}, u32[]{:S(2)}, u32[]{:S(2)}) %collective-permute-start.12) | collective-permute-done | bytes 589856 | tf_op jit(solution)/shard_map/ppermute | solution.py:280
  120.9 2.4 %collective-permute-start.15 = (f32[32,1152]{1,0:T(8,128)S(1)}, f32[32,1152]{1,0:T(8,128)S(1)}, u32[]{:S(2)}, u32[]{:S(2)}) collective-permute-start(f32[32,1152]{1,0:T(8,128)S(1)} %get-tuple-element.22), channel_id=1, source_target_pairs={{0,12},{1,13},{2,14},{3,15},{4,8},{5,9},{6,10},{7,11},{8,4},{9,5},... | collective-permute-start | bytes 442376 | tf_op jit(solution)/shard_map/ppermute | solution.py:280
  123.8 1.3 collective-permute-done.13
  125.1 6.1 %collective-permute-done.15 = f32[32,1152]{1,0:T(8,128)S(1)} collective-permute-done((f32[32,1152]{1,0:T(8,128)S(1)}, f32[32,1152]{1,0:T(8,128)S(1)}, u32[]{:S(2)}, u32[]{:S(2)}) %collective-permute-start.15) | collective-permute-done | bytes 147488 | tf_op jit(solution)/shard_map/ppermute | solution.py:280
  131.2 5.1 %collective-permute-done.14 = f32[32,1152]{1,0:T(8,128)S(1)} collective-permute-done((f32[32,1152]{1,0:T(8,128)S(1)}, f32[32,1152]{1,0:T(8,128)S(1)}, u32[]{:S(2)}, u32[]{:S(2)}) %collective-permute-start.14) | collective-permute-done | bytes 147488 | tf_op jit(solution)/shard_map/ppermute | solution.py:280
  136.3 3.4 %collective-permute-start.18 = (f32[32,1152]{1,0:T(8,128)S(1)}, f32[32,1152]{1,0:T(8,128)S(1)}, u32[]{:S(2)}, u32[]{:S(2)}) collective-permute-start(f32[32,1152]{1,0:T(8,128)S(1)} %fusion.2), channel_id=1, source_target_pairs={{0,12},{1,13},{2,14},{3,15},{4,8},{5,9},{6,10},{7,11},{8,4},{9,5},... | collective-permute-start | bytes 442376 | tf_op jit(solution)/shard_map/ppermute | solution.py:280
  140.8 4.2 %collective-permute-done.18 = f32[32,1152]{1,0:T(8,128)S(1)} collective-permute-done((f32[32,1152]{1,0:T(8,128)S(1)}, f32[32,1152]{1,0:T(8,128)S(1)}, u32[]{:S(2)}, u32[]{:S(2)}) %collective-permute-start.18) | collective-permute-done | bytes 147488 | tf_op jit(solution)/shard_map/ppermute | solution.py:280
  145.0 5.6 %collective-permute-done.17 = f32[32,1152]{1,0:T(8,128)S(1)} collective-permute-done((f32[32,1152]{1,0:T(8,128)S(1)}, f32[32,1152]{1,0:T(8,128)S(1)}, u32[]{:S(2)}, u32[]{:S(2)}) %collective-permute-start.17) | collective-permute-done | bytes 147488 | tf_op jit(solution)/shard_map/ppermute | solution.py:280
  151.8 12.7 %collective-permute-done.19.refs_1_ = f32[128,1152]{1,0:T(8,128)S(1)} collective-permute-done((f32[128,1152]{1,0:T(8,128)S(1)}, f32[128,1152]{1,0:T(8,128)S(1)}, u32[]{:S(2)}, u32[]{:S(2)}) %collective-permute-start.19) | collective-permute-done | bytes 589856 | tf_op jit(solution)/shard_map/ppermute | solution.py:280
  164.6 17.4 %shard_map.60.refs_5_ = f32[1024,1024]{1,0:T(8,128)S(1)} custom-call(f32[1024,1024]{1,0:T(8,128)} %x_ref.1, bf16[1024,1024]{1,0:T(8,128)(2,1)S(1)} %get-tuple-element.15.hi_ref, bf16[1024,1024]{1,0:T(8,128)(2,1)S(1)} %get-tuple-element.16.lo_ref, f32[1024,1024]{1,0:T(8,128)} %copy-done.4, f32[1024,1024]{1,0:T(8,128)} %s_ref.1), custom_call_target="tpu_custom_call" | custom-call | flops 12884901888 | bytes 20971520 | tf_op jit(solution)/shard_map/pallas_call | solution.py:221
  182.0 1.9 %copy-done.3 = f32[1024,1024]{1,0:T(8,128)} copy-done((f32[1024,1024]{1,0:T(8,128)}, f32[1024,1024]{1,0:T(8,128)S(1)}, u32[]{:S(2)}) %copy-start.3) | copy-done | bytes 4194328
  184.0 10.4 %shard_map.61 = f32[1024,1024]{1,0:T(8,128)} custom-call(s32[1]{0:T(128)} %bitcast.me_ref, f32[128,1152]{1,0:T(8,128)S(1)} %pad_maximum_fusion.1.refs_0_, f32[128,1152]{1,0:T(8,128)S(1)} %collective-permute-done.19.refs_1_, f32[128,1152]{1,0:T(8,128)S(1)} %collective-permute-done.20.refs_2_, f32[128,1152]{1,0:T(8,128)S(1)} %collective-permute-done.21.refs_3_, ...), custom_call_target="tpu_custom_call" | custom-call | flops 6442450944 | bytes 16777216 | tf_op jit(solution)/shard_map/pallas_call | solution.py:247
  (41 shorter events, 8.0 us)
Async XLA Ops:
  0.0 2.2 %copy-start.1 = (f32[1024,1024]{1,0:T(8,128)S(1)}, f32[1024,1024]{1,0:T(8,128)}, u32[]{:S(2)}) copy-start(f32[1024,1024]{1,0:T(8,128)} %x_ref.1) | copy-start | bytes 12582916
  12.1 3.0 %collective-permute-start = (f32[256,1152]{1,0:T(8,128)S(1)}, f32[256,1152]{1,0:T(8,128)S(1)}, u32[]{:S(2)}, u32[]{:S(2)}) collective-permute-start(f32[256,1152]{1,0:T(8,128)S(1)} %get-tuple-element.12), channel_id=1, source_target_pairs={{0,1},{1,0},{2,3},{3,2},{4,5},{5,4},{6,7},{7,6},{8,9},{9,8},{10,11... | collective-permute-start | bytes 3538952 | tf_op jit(solution)/shard_map/ppermute | solution.py:280
  15.0 38.3 %copy-start = (f32[1024,1024]{1,0:T(8,128)S(1)}, f32[1024,1024]{1,0:T(8,128)}, u32[]{:S(2)}) copy-start(f32[1024,1024]{1,0:T(8,128)} %a_ref.6) | copy-start | bytes 12582916
  15.2 16.6 %collective-permute-start.1 = (f32[128,1152]{1,0:T(8,128)S(1)}, f32[128,1152]{1,0:T(8,128)S(1)}, u32[]{:S(2)}, u32[]{:S(2)}) collective-permute-start(f32[128,1152]{1,0:T(8,128)S(1)} %get-tuple-element.20), channel_id=1, source_target_pairs={{0,2},{1,3},{2,0},{3,1},{4,6},{5,7},{6,4},{7,5},{8,10},{9,11},{10,... | collective-permute-start | bytes 1769480 | tf_op jit(solution)/shard_map/ppermute | solution.py:280
  31.8 5.6 %collective-permute-start.2 = (f32[32,1152]{1,0:T(8,128)S(1)}, f32[32,1152]{1,0:T(8,128)S(1)}, u32[]{:S(2)}, u32[]{:S(2)}) collective-permute-start(f32[32,1152]{1,0:T(8,128)S(1)} %get-tuple-element.24), channel_id=1, source_target_pairs={{0,4},{1,5},{2,6},{3,7},{4,0},{5,1},{6,2},{7,3},{8,12},{9,13},{10,... | collective-permute-start | bytes 442376 | tf_op jit(solution)/shard_map/ppermute | solution.py:280
  33.7 10.3 %collective-permute-start.4 = (f32[32,1152]{1,0:T(8,128)S(1)}, f32[32,1152]{1,0:T(8,128)S(1)}, u32[]{:S(2)}, u32[]{:S(2)}) collective-permute-start(f32[32,1152]{1,0:T(8,128)S(1)} %get-tuple-element.25), channel_id=1, source_target_pairs={{0,12},{1,13},{2,14},{3,15},{4,8},{5,9},{6,10},{7,11},{8,4},{9,5},... | collective-permute-start | bytes 442376 | tf_op jit(solution)/shard_map/ppermute | solution.py:280
  36.2 12.6 %collective-permute-start.3 = (f32[32,1152]{1,0:T(8,128)S(1)}, f32[32,1152]{1,0:T(8,128)S(1)}, u32[]{:S(2)}, u32[]{:S(2)}) collective-permute-start(f32[32,1152]{1,0:T(8,128)S(1)} %get-tuple-element.26), channel_id=1, source_target_pairs={{0,8},{1,9},{2,10},{3,11},{4,12},{5,13},{6,14},{7,15},{8,0},{9,1},... | collective-permute-start | bytes 442376 | tf_op jit(solution)/shard_map/ppermute | solution.py:280
  48.9 18.2 %copy-start.2 = (f32[1024,1024]{1,0:T(8,128)S(1)}, f32[1024,1024]{1,0:T(8,128)}, u32[]{:S(2)}) copy-start(f32[1024,1024]{1,0:T(8,128)} %refs_4_.1) | copy-start | bytes 12582916
  48.9 16.5 %collective-permute-start.7 = (f32[32,1152]{1,0:T(8,128)S(1)}, f32[32,1152]{1,0:T(8,128)S(1)}, u32[]{:S(2)}, u32[]{:S(2)}) collective-permute-start(f32[32,1152]{1,0:T(8,128)S(1)} %fusion.5), channel_id=1, source_target_pairs={{0,12},{1,13},{2,14},{3,15},{4,8},{5,9},{6,10},{7,11},{8,4},{9,5},... | collective-permute-start | bytes 442376 | tf_op jit(solution)/shard_map/ppermute | solution.py:280
  52.3 13.2 %collective-permute-start.6 = (f32[32,1152]{1,0:T(8,128)S(1)}, f32[32,1152]{1,0:T(8,128)S(1)}, u32[]{:S(2)}, u32[]{:S(2)}) collective-permute-start(f32[32,1152]{1,0:T(8,128)S(1)} %fusion.5), channel_id=1, source_target_pairs={{0,8},{1,9},{2,10},{3,11},{4,12},{5,13},{6,14},{7,15},{8,0},{9,1},... | collective-permute-start | bytes 442376 | tf_op jit(solution)/shard_map/ppermute | solution.py:280
  52.3 13.2 %collective-permute-start.5 = (f32[32,1152]{1,0:T(8,128)S(1)}, f32[32,1152]{1,0:T(8,128)S(1)}, u32[]{:S(2)}, u32[]{:S(2)}) collective-permute-start(f32[32,1152]{1,0:T(8,128)S(1)} %fusion.5), channel_id=1, source_target_pairs={{0,4},{1,5},{2,6},{3,7},{4,0},{5,1},{6,2},{7,3},{8,12},{9,13},{10,... | collective-permute-start | bytes 442376 | tf_op jit(solution)/shard_map/ppermute | solution.py:280
  63.5 2.0 %copy-start.4 = (f32[1024,1024]{1,0:T(8,128)}, f32[1024,1024]{1,0:T(8,128)S(1)}, u32[]{:S(2)}) copy-start(f32[1024,1024]{1,0:T(8,128)S(1)} %shard_map.57.b_ref.m_ref) | copy-start | bytes 12582916
  65.5 13.2 %collective-permute-start.8 = (f32[128,1152]{1,0:T(8,128)S(1)}, f32[128,1152]{1,0:T(8,128)S(1)}, u32[]{:S(2)}, u32[]{:S(2)}) collective-permute-start(f32[128,1152]{1,0:T(8,128)S(1)} %pad_maximum_fusion.refs_0_), channel_id=1, source_target_pairs={{0,2},{1,3},{2,0},{3,1},{4,6},{5,7},{6,4},{7,5},{8,10},{9,11},{10,... | collective-permute-start | bytes 1769480 | tf_op jit(solution)/shard_map/ppermute | solution.py:280
  76.5 2.0 %copy-start.5 = (f32[1024,1024]{1,0:T(8,128)}, f32[1024,1024]{1,0:T(8,128)S(1)}, u32[]{:S(2)}) copy-start(f32[1024,1024]{1,0:T(8,128)S(1)} %shard_map.56.refs_4_) | copy-start | bytes 12582916
  78.5 11.9 %collective-permute-start.9 = (f32[128,1152]{1,0:T(8,128)S(1)}, f32[128,1152]{1,0:T(8,128)S(1)}, u32[]{:S(2)}, u32[]{:S(2)}) collective-permute-start(f32[128,1152]{1,0:T(8,128)S(1)} %pad_maximum_fusion.refs_0_), channel_id=1, source_target_pairs={{0,1},{1,0},{2,3},{3,2},{4,5},{5,4},{6,7},{7,6},{8,9},{9,8},{10,11... | collective-permute-start | bytes 1769480 | tf_op jit(solution)/shard_map/ppermute | solution.py:280
  78.7 11.8 %collective-permute-start.10 = (f32[128,1152]{1,0:T(8,128)S(1)}, f32[128,1152]{1,0:T(8,128)S(1)}, u32[]{:S(2)}, u32[]{:S(2)}) collective-permute-start(f32[128,1152]{1,0:T(8,128)S(1)} %collective-permute-done.8.refs_1_), channel_id=1, source_target_pairs={{0,1},{1,0},{2,3},{3,2},{4,5},{5,4},{6,7},{7,6},{8,9},{9,8},{10,11... | collective-permute-start | bytes 1769480 | tf_op jit(solution)/shard_map/ppermute | solution.py:280
  88.4 2.0 %copy-start.6 = (f32[1024,1024]{1,0:T(8,128)}, f32[1024,1024]{1,0:T(8,128)S(1)}, u32[]{:S(2)}) copy-start(f32[1024,1024]{1,0:T(8,128)S(1)} %shard_map.58.refs_5_) | copy-start | bytes 12582916
  101.3 2.9 %collective-permute-start.11 = (f32[256,1152]{1,0:T(8,128)S(1)}, f32[256,1152]{1,0:T(8,128)S(1)}, u32[]{:S(2)}, u32[]{:S(2)}) collective-permute-start(f32[256,1152]{1,0:T(8,128)S(1)} %get-tuple-element.14), channel_id=1, source_target_pairs={{0,1},{1,0},{2,3},{3,2},{4,5},{5,4},{6,7},{7,6},{8,9},{9,8},{10,11... | collective-permute-start | bytes 3538952 | tf_op jit(solution)/shard_map/ppermute | solution.py:280
  104.3 15.5 %collective-permute-start.12 = (f32[128,1152]{1,0:T(8,128)S(1)}, f32[128,1152]{1,0:T(8,128)S(1)}, u32[]{:S(2)}, u32[]{:S(2)}) collective-permute-start(f32[128,1152]{1,0:T(8,128)S(1)} %get-tuple-element.18), channel_id=1, source_target_pairs={{0,2},{1,3},{2,0},{3,1},{4,6},{5,7},{6,4},{7,5},{8,10},{9,11},{10,... | collective-permute-start | bytes 1769480 | tf_op jit(solution)/shard_map/ppermute | solution.py:280
  119.9 5.2 %collective-permute-start.13 = (f32[32,1152]{1,0:T(8,128)S(1)}, f32[32,1152]{1,0:T(8,128)S(1)}, u32[]{:S(2)}, u32[]{:S(2)}) collective-permute-start(f32[32,1152]{1,0:T(8,128)S(1)} %get-tuple-element.21), channel_id=1, source_target_pairs={{0,4},{1,5},{2,6},{3,7},{4,0},{5,1},{6,2},{7,3},{8,12},{9,13},{10,... | collective-permute-start | bytes 442376 | tf_op jit(solution)/shard_map/ppermute | solution.py:280
  120.9 10.3 %collective-permute-start.15 = (f32[32,1152]{1,0:T(8,128)S(1)}, f32[32,1152]{1,0:T(8,128)S(1)}, u32[]{:S(2)}, u32[]{:S(2)}) collective-permute-start(f32[32,1152]{1,0:T(8,128)S(1)} %get-tuple-element.22), channel_id=1, source_target_pairs={{0,12},{1,13},{2,14},{3,15},{4,8},{5,9},{6,10},{7,11},{8,4},{9,5},... | collective-permute-start | bytes 442376 | tf_op jit(solution)/shard_map/ppermute | solution.py:280
  123.3 13.0 %collective-permute-start.14 = (f32[32,1152]{1,0:T(8,128)S(1)}, f32[32,1152]{1,0:T(8,128)S(1)}, u32[]{:S(2)}, u32[]{:S(2)}) collective-permute-start(f32[32,1152]{1,0:T(8,128)S(1)} %get-tuple-element.23), channel_id=1, source_target_pairs={{0,8},{1,9},{2,10},{3,11},{4,12},{5,13},{6,14},{7,15},{8,0},{9,1},... | collective-permute-start | bytes 442376 | tf_op jit(solution)/shard_map/ppermute | solution.py:280
  136.3 8.7 %collective-permute-start.18 = (f32[32,1152]{1,0:T(8,128)S(1)}, f32[32,1152]{1,0:T(8,128)S(1)}, u32[]{:S(2)}, u32[]{:S(2)}) collective-permute-start(f32[32,1152]{1,0:T(8,128)S(1)} %fusion.2), channel_id=1, source_target_pairs={{0,12},{1,13},{2,14},{3,15},{4,8},{5,9},{6,10},{7,11},{8,4},{9,5},... | collective-permute-start | bytes 442376 | tf_op jit(solution)/shard_map/ppermute | solution.py:280
  139.7 10.9 %collective-permute-start.17 = (f32[32,1152]{1,0:T(8,128)S(1)}, f32[32,1152]{1,0:T(8,128)S(1)}, u32[]{:S(2)}, u32[]{:S(2)}) collective-permute-start(f32[32,1152]{1,0:T(8,128)S(1)} %fusion.2), channel_id=1, source_target_pairs={{0,8},{1,9},{2,10},{3,11},{4,12},{5,13},{6,14},{7,15},{8,0},{9,1},... | collective-permute-start | bytes 442376 | tf_op jit(solution)/shard_map/ppermute | solution.py:280
  139.7 10.9 %collective-permute-start.16 = (f32[32,1152]{1,0:T(8,128)S(1)}, f32[32,1152]{1,0:T(8,128)S(1)}, u32[]{:S(2)}, u32[]{:S(2)}) collective-permute-start(f32[32,1152]{1,0:T(8,128)S(1)} %fusion.2), channel_id=1, source_target_pairs={{0,4},{1,5},{2,6},{3,7},{4,0},{5,1},{6,2},{7,3},{8,12},{9,13},{10,... | collective-permute-start | bytes 442376 | tf_op jit(solution)/shard_map/ppermute | solution.py:280
  150.6 13.9 %collective-permute-start.19 = (f32[128,1152]{1,0:T(8,128)S(1)}, f32[128,1152]{1,0:T(8,128)S(1)}, u32[]{:S(2)}, u32[]{:S(2)}) collective-permute-start(f32[128,1152]{1,0:T(8,128)S(1)} %pad_maximum_fusion.1.refs_0_), channel_id=1, source_target_pairs={{0,2},{1,3},{2,0},{3,1},{4,6},{5,7},{6,4},{7,5},{8,10},{9,11},{10,... | collective-permute-start | bytes 1769480 | tf_op jit(solution)/shard_map/ppermute | solution.py:280
  151.8 32.1 %collective-permute-start.20 = (f32[128,1152]{1,0:T(8,128)S(1)}, f32[128,1152]{1,0:T(8,128)S(1)}, u32[]{:S(2)}, u32[]{:S(2)}) collective-permute-start(f32[128,1152]{1,0:T(8,128)S(1)} %pad_maximum_fusion.1.refs_0_), channel_id=1, source_target_pairs={{0,1},{1,0},{2,3},{3,2},{4,5},{5,4},{6,7},{7,6},{8,9},{9,8},{10,11... | collective-permute-start | bytes 1769480 | tf_op jit(solution)/shard_map/ppermute | solution.py:280
  164.6 19.4 %collective-permute-start.21 = (f32[128,1152]{1,0:T(8,128)S(1)}, f32[128,1152]{1,0:T(8,128)S(1)}, u32[]{:S(2)}, u32[]{:S(2)}) collective-permute-start(f32[128,1152]{1,0:T(8,128)S(1)} %collective-permute-done.19.refs_1_), channel_id=1, source_target_pairs={{0,1},{1,0},{2,3},{3,2},{4,5},{5,4},{6,7},{7,6},{8,9},{9,8},{10,11... | collective-permute-start | bytes 1769480 | tf_op jit(solution)/shard_map/ppermute | solution.py:280
  182.0 2.0 %copy-start.3 = (f32[1024,1024]{1,0:T(8,128)}, f32[1024,1024]{1,0:T(8,128)S(1)}, u32[]{:S(2)}) copy-start(f32[1024,1024]{1,0:T(8,128)S(1)} %shard_map.60.refs_5_) | copy-start | bytes 12582916
